TPU v7x, 32 devices: a whole 2x2x4 slice. The times are simulated.
32 devices in a mesh: groups: 2 (over x), own: 16 (over z, y, core).
Axes of the slice: x: 2, y: 2, z: 4, core: 2. Of those that a mesh axis runs over, the one named last changes fastest.
Arguments:
- embeddings: bfloat16 [512, 128, 1280], P(('groups', 'own')), parts along dimension 0, may hold values from -24 to 24
- lengths: int32 [512], P('groups'), parts along dimension 0, may hold values from 1 to 128, 16384 in all
- proj_weight: bfloat16 [1280, 1280], replicated, may hold values from -0.15625 to 0.15625
- slot_of: int32 [512], P('groups'), parts along dimension 0, may hold values from 0 to 255, as said below
- pairs: int32 [768, 2], P(('groups', 'own')), parts along dimension 0, may hold values from 0 to 255, as said below
Outputs:
- interface: float32 [512, 20, 128], P(('groups', 'own')), parts along dimension 0
There are 2 independent parts, one for each index of `groups`. A program takes and returns all parts, laid end to end along the dimension named above; an argument that names none is the same for every part. Nothing has to cross between parts.
Inputs may be any that keep to these rules, and one draw needn't show every extreme that they name: A permutation: protein p is stored in row slot_of[p] of embeddings, on index slot_of[p] // 16 of own. Pair r is held by the owner of its first protein: slot_of[pairs[r, 0]] // 16 == r // 24. The second proteins of one device's 24 pairs are distinct, at most 2 of them stored on any one owner, and every device has some owner that stores exactly 2 of them. A pair may name one protein twice.
All inputs are finite; a program needn't handle non-finite values.
Results may differ from a plain program's by a relative error of at most 0.007.
Values may be sent and summed in bfloat16 or wider, within the bound.
A program may use at most 128 MiB of HBM per device.

v0:
```python
import math

import jax
import jax.numpy as jnp
from jax import lax
from jax.sharding import PartitionSpec as P

HEADS = 20
CAP = 2


block_pairs = 8


def pair_mass(query, partner, len_query, len_partner):
    batch, residues, channels = query.shape
    head_size = channels // HEADS
    left = query.reshape(batch, residues, HEADS, head_size)
    right = partner.reshape(batch, residues, HEADS, head_size)
    scores = jnp.einsum(
        "bihe,bjhe->bhij", left, right, preferred_element_type=jnp.float32
    ) / math.sqrt(head_size)
    positions = jnp.arange(residues, dtype=jnp.int32)
    rows_live = positions[None, :] < len_query[:, None]
    cols_live = positions[None, :] < len_partner[:, None]
    live = rows_live[:, None, :, None] & cols_live[:, None, None, :]
    masked = jnp.where(live, scores, -1e30)
    row_top = jnp.max(masked, axis=3, keepdims=True)
    row_exp = jnp.where(live, jnp.exp(masked - row_top), 0.0)
    row_total = (
        jnp.sum(row_exp, axis=3, keepdims=True) + jnp.where(rows_live, 0.0, 1.0)[:, None, :, None]
    )
    to_partner = jnp.sum(row_exp / row_total, axis=2)
    col_top = jnp.max(masked, axis=2, keepdims=True)
    col_exp = jnp.where(live, jnp.exp(masked - col_top), 0.0)
    col_total = (
        jnp.sum(col_exp, axis=2, keepdims=True) + jnp.where(cols_live, 0.0, 1.0)[:, None, None, :]
    )
    to_query = jnp.sum(col_exp / col_total, axis=3)
    ratio = len_partner.astype(jnp.float32) / len_query.astype(jnp.float32)
    return (to_query / ratio[:, None, None], to_partner * ratio[:, None, None])


def local(embeddings, lengths, proj_weight, slot_of, pairs):
    per_device, residues, channels = embeddings.shape
    owners = lax.axis_size("own")
    own_index = lax.axis_index("own")
    pair_count = pairs.shape[0]
    row_first = jnp.take(slot_of, pairs[:, 0])
    row_second = jnp.take(slot_of, pairs[:, 1])
    len_first = jnp.take(lengths, pairs[:, 0])
    len_second = jnp.take(lengths, pairs[:, 1])
    local_first = row_first - own_index * per_device
    holder_second = row_second // per_device
    local_second = row_second % per_device
    order_ids = jnp.arange(pair_count, dtype=jnp.int32)
    earlier = (holder_second[:, None] == holder_second[None, :]) & (
        order_ids[None, :] < order_ids[:, None]
    )
    rank = jnp.sum(earlier.astype(jnp.int32), axis=1)
    placed = holder_second * CAP + rank
    slot_count = owners * CAP
    slot_ids = jnp.arange(slot_count, dtype=jnp.int32)
    wanted = (
        jnp.sum(
            jnp.where(placed[:, None] == slot_ids[None, :], local_second[:, None] + 1, 0), axis=0
        )
        - 1
    )
    asked = lax.all_to_all(
        wanted.reshape(owners, CAP), "own", split_axis=0, concat_axis=0, tiled=True
    ).reshape(slot_count)
    features = jnp.dot(
        embeddings.reshape(per_device * residues, channels),
        proj_weight,
        preferred_element_type=jnp.float32,
    )
    features = features.astype(jnp.bfloat16).reshape(per_device, residues, channels)
    outgoing = jnp.take(features, jnp.maximum(asked, 0), axis=0)
    arrived = lax.all_to_all(
        outgoing.reshape(owners, CAP, residues, channels),
        "own",
        split_axis=0,
        concat_axis=0,
        tiled=True,
    )
    arrived = arrived.reshape(slot_count, residues, channels)
    device_rows = jnp.arange(per_device, dtype=jnp.int32)

    def step(carry, item):
        own_total, slot_total = carry
        first_local, slot_place, first_len, second_len = item
        query = jnp.take(features, first_local, axis=0)
        partner = jnp.take(arrived, slot_place, axis=0)
        to_query, to_partner = pair_mass(query, partner, first_len, second_len)
        own_hits = (first_local[:, None] == device_rows[None, :]).astype(jnp.float32)
        slot_hits = (slot_place[:, None] == slot_ids[None, :]).astype(jnp.float32)
        own_total = own_total + jnp.einsum(
            "bp,bhl->phl", own_hits, to_query, precision=lax.Precision.HIGHEST
        )
        slot_total = slot_total + jnp.einsum(
            "bs,bhl->shl", slot_hits, to_partner, precision=lax.Precision.HIGHEST
        )
        return ((own_total, slot_total), None)

    blocks = pair_count // block_pairs
    items = (
        local_first.reshape(blocks, block_pairs),
        placed.reshape(blocks, block_pairs),
        len_first.reshape(blocks, block_pairs),
        len_second.reshape(blocks, block_pairs),
    )
    start = (
        jnp.zeros((per_device, HEADS, residues), jnp.float32),
        jnp.zeros((slot_count, HEADS, residues), jnp.float32),
    )
    (own_total, slot_total), _ = lax.scan(step, start, items)
    slot_rows = slot_ids // CAP * per_device + wanted
    all_rows = jnp.arange(owners * per_device, dtype=jnp.int32)
    row_hits = ((slot_rows[:, None] == all_rows[None, :]) & (wanted >= 0)[:, None]).astype(
        jnp.float32
    )
    spread = jnp.einsum("sr,shl->rhl", row_hits, slot_total, precision=lax.Precision.HIGHEST)
    return own_total + lax.psum_scatter(spread, "own", scatter_dimension=0, tiled=True)


def solution(mesh):
    placed = (
        P(("groups", "own"), None, None),
        P("groups"),
        P(),
        P("groups"),
        P(("groups", "own"), None),
    )
    return jax.shard_map(
        local,
        mesh=mesh,
        in_specs=placed,
        out_specs=P(("groups", "own"), None, None),
        check_vma=False,
    )
```

profile of v0, /device:TPU:0, one launch (start us, length us, event | category | flops | bytes accessed | tf_op | source)
XLA Modules:
  0.0 575.2 jit_solution(16358287095289050426)
XLA Ops:
  15.4 7.4 %all-to-all-start = ((s32[16,1,2]{2,1,0:T(1,128)}), s32[16,1,2]{2,1,0:T(1,128)S(1)}, u32[]{:S(2)}, u32[]{:S(2)}) async-start(s32[16,1,2]{2,1,0:T(1,128)} %bitcast.4), calls=%async_computation | async-start | bytes 16384 | tf_op jit(solution)/shard_map/all_to_all | solution.py:70
  22.8 10.3 %convolution_convert_fusion = bf16[2048,1280]{1,0:T(8,128)(2,1)} fusion(bf16[2048,1280]{1,0:T(8,128)(2,1)} %bitcast.66, bf16[1280,1280]{1,0:T(8,128)(2,1)S(1)} %copy-done), kind=kOutput, calls=%fused_computation.68 | convolution fusion | flops 6713507840 | bytes 13762560 | tf_op jit(solution)/shard_map/dot_general | solution.py:73
  33.5 8.4 %gather_fusion.2 = bf16[32,128,1280]{2,1,0:T(8,128)(2,1)} fusion(bf16[16,128,1280]{2,1,0:T(8,128)(2,1)} %bitcast.62, s32[1024]{0:T(1024)S(1)} %pad_clamp_fusion.2), kind=kCustom, calls=%fused_computation.6 | custom fusion | bytes 20971648 | tf_op jit(solution)/shard_map/jit(_take)/gather | solution.py:79
  42.0 10.1 %broadcast_select_fusion.2 = bf16[16,2,128,1280]{3,2,1,0:T(8,128)(2,1)} fusion(bf16[16,2,128,1280]{3,2,1,0:T(8,128)(2,1)} %bitcast.64, pred[16,2]{1,0:T(8,128)(4,1)S(1)} %copy.36), kind=kLoop, calls=%fused_computation.67 | loop fusion | flops 5242880 | bytes 20971552 | tf_op jit(solution)/shard_map/jit(_take)/select_n | solution.py:79
  52.1 6.1 %all-to-all-start.1 = ((bf16[16,2,128,1280]{3,2,1,0:T(8,128)(2,1)}), bf16[16,2,128,1280]{3,2,1,0:T(8,128)(2,1)}, u32[]{:S(2)}, u32[]{:S(2)}) async-start(bf16[16,2,128,1280]{3,2,1,0:T(8,128)(2,1)} %broadcast_select_fusion.2), calls=%async_computation.1 | async-start | bytes 20971520 | tf_op jit(solution)/shard_map/all_to_all | solution.py:80
  59.2 186.3 %all-to-all-done.1 = bf16[16,2,128,1280]{3,2,1,0:T(8,128)(2,1)} async-done(((bf16[16,2,128,1280]{3,2,1,0:T(8,128)(2,1)}), bf16[16,2,128,1280]{3,2,1,0:T(8,128)(2,1)}, u32[]{:S(2)}, u32[]{:S(2)}) %all-to-all-start.1) | async-done | bytes 10485792 | tf_op jit(solution)/shard_map/all_to_all | solution.py:80
  245.4 213.2 %while.13 = (s32[]{:T(128)}, f32[16,20,128]{2,0,1:T(8,128)S(1)}, f32[32,20,128]{2,0,1:T(8,128)}, s32[3,8]{1,0:T(4,128)S(1)}, s32[3,8]{1,0:T(4,128)S(1)}, /*index...) while((s32[]{:T(128)}, f32[16,20,128]{2,0,1:T(8,128)S(1)}, ...), condition=%wide.region_9.11_spmd.clone, body=%wide.region_2.10_spmd.clone.sunk | while | flops 392332096 | bytes 102003648 | solution.py:117
  245.5 4.7 gather_fusion
  258.6 8.1 %fusion.65 = f32[8,20,128,128]{3,2,1,0:T(8,128)} fusion(bf16[8,128,20,64]{1,3,2,0:T(8,128)(2,1)} %bitcast.60, bf16[8,128,20,64]{1,3,2,0:T(8,128)(2,1)} %bitcast.61, pred[8]{0:T(512)(128)(4,1)S(1)} %get-tuple-element.220, pred[8]{0:T(512)(128)(4,1)S(1)} %get-tuple-element.221), kind=kOutput, calls=%fused_computation.18.clone.1 | convolution fusion | flops 338165760 | bytes 15728656 | tf_op jit(solution)/shard_map/while/body/eval_jaxpr/bihe,bjhe->bhij/dot_general | solution.py:20
  267.1 16.4 %fusion.67 = (f32[8,20,128]{2,1,0:T(8,128)S(1)}, f32[8,20,128,128]{3,2,1,0:T(8,128)}) fusion(f32[8,20,128,128]{3,2,1,0:T(8,128)} %fusion.65, pred[8,128,128]{2,1,0:T(8,128)(4,1)S(1)} %broadcast_and_fusion.2), kind=kOutput, calls=%fused_computation.109.clone.1 | output fusion | flops 18350208 | bytes 21184512 | tf_op jit(solution)/shard_map/while/body/eval_jaxpr/sub | solution.py:29
  283.6 6.7 %divide_reduce_fusion.5 = f32[8,20,128]{2,1,0:T(8,128)S(1)} fusion(f32[8,20,128,128]{3,2,1,0:T(8,128)} %get-tuple-element.231, f32[8,20,128]{2,1,0:T(8,128)S(1)} %broadcast_add_fusion.6), kind=kLoop, calls=%fused_computation.14.clone.1 | loop fusion | flops 5222400 | bytes 10649600 | tf_op jit(solution)/shard_map/while/body/eval_jaxpr/reduce_sum | solution.py:33
  291.5 17.3 %fusion.66 = (f32[8,20,128]{2,1,0:T(8,128)S(1)}, f32[8,20,128,128]{3,2,1,0:T(8,128)}) fusion(f32[8,20,128,128]{3,2,1,0:T(8,128)} %fusion.65, pred[8,128,128]{2,1,0:T(8,128)(4,1)S(1)} %broadcast_and_fusion.2), kind=kOutput, calls=%fused_computation.108.clone.1 | output fusion | flops 13107327 | bytes 21184512 | tf_op jit(solution)/shard_map/while/body/eval_jaxpr/sub | solution.py:35
  308.7 6.8 %divide_reduce_fusion.4 = f32[8,20,128]{2,1,0:T(8,128)S(1)} fusion(f32[8,20,128,128]{3,2,1,0:T(8,128)} %get-tuple-element.226, f32[8,20,128]{2,1,0:T(8,128)S(1)} %broadcast_add_fusion.5), kind=kLoop, calls=%fused_computation.15.clone.1 | loop fusion | flops 5222400 | bytes 10649600 | tf_op jit(solution)/shard_map/while/body/eval_jaxpr/reduce_sum | solution.py:39
  329.1 8.1 %fusion.65 = f32[8,20,128,128]{3,2,1,0:T(8,128)} fusion(bf16[8,128,20,64]{1,3,2,0:T(8,128)(2,1)} %bitcast.60, bf16[8,128,20,64]{1,3,2,0:T(8,128)(2,1)} %bitcast.61, pred[8]{0:T(512)(128)(4,1)S(1)} %get-tuple-element.220, pred[8]{0:T(512)(128)(4,1)S(1)} %get-tuple-element.221), kind=kOutput, calls=%fused_computation.18.clone.1 | convolution fusion | flops 338165760 | bytes 15728656 | tf_op jit(solution)/shard_map/while/body/eval_jaxpr/bihe,bjhe->bhij/dot_general | solution.py:20
  337.5 16.4 %fusion.67 = (f32[8,20,128]{2,1,0:T(8,128)S(1)}, f32[8,20,128,128]{3,2,1,0:T(8,128)}) fusion(f32[8,20,128,128]{3,2,1,0:T(8,128)} %fusion.65, pred[8,128,128]{2,1,0:T(8,128)(4,1)S(1)} %broadcast_and_fusion.2), kind=kOutput, calls=%fused_computation.109.clone.1 | output fusion | flops 18350208 | bytes 21184512 | tf_op jit(solution)/shard_map/while/body/eval_jaxpr/sub | solution.py:29
  354.0 6.7 %divide_reduce_fusion.5 = f32[8,20,128]{2,1,0:T(8,128)S(1)} fusion(f32[8,20,128,128]{3,2,1,0:T(8,128)} %get-tuple-element.231, f32[8,20,128]{2,1,0:T(8,128)S(1)} %broadcast_add_fusion.6), kind=kLoop, calls=%fused_computation.14.clone.1 | loop fusion | flops 5222400 | bytes 10649600 | tf_op jit(solution)/shard_map/while/body/eval_jaxpr/reduce_sum | solution.py:33
  362.8 17.3 %fusion.66 = (f32[8,20,128]{2,1,0:T(8,128)S(1)}, f32[8,20,128,128]{3,2,1,0:T(8,128)}) fusion(f32[8,20,128,128]{3,2,1,0:T(8,128)} %fusion.65, pred[8,128,128]{2,1,0:T(8,128)(4,1)S(1)} %broadcast_and_fusion.2), kind=kOutput, calls=%fused_computation.108.clone.1 | output fusion | flops 13107327 | bytes 21184512 | tf_op jit(solution)/shard_map/while/body/eval_jaxpr/sub | solution.py:35
  380.1 6.8 %divide_reduce_fusion.4 = f32[8,20,128]{2,1,0:T(8,128)S(1)} fusion(f32[8,20,128,128]{3,2,1,0:T(8,128)} %get-tuple-element.226, f32[8,20,128]{2,1,0:T(8,128)S(1)} %broadcast_add_fusion.5), kind=kLoop, calls=%fused_computation.15.clone.1 | loop fusion | flops 5222400 | bytes 10649600 | tf_op jit(solution)/shard_map/while/body/eval_jaxpr/reduce_sum | solution.py:39
  400.4 8.1 %fusion.65 = f32[8,20,128,128]{3,2,1,0:T(8,128)} fusion(bf16[8,128,20,64]{1,3,2,0:T(8,128)(2,1)} %bitcast.60, bf16[8,128,20,64]{1,3,2,0:T(8,128)(2,1)} %bitcast.61, pred[8]{0:T(512)(128)(4,1)S(1)} %get-tuple-element.220, pred[8]{0:T(512)(128)(4,1)S(1)} %get-tuple-element.221), kind=kOutput, calls=%fused_computation.18.clone.1 | convolution fusion | flops 338165760 | bytes 15728656 | tf_op jit(solution)/shard_map/while/body/eval_jaxpr/bihe,bjhe->bhij/dot_general | solution.py:20
  408.9 16.4 %fusion.67 = (f32[8,20,128]{2,1,0:T(8,128)S(1)}, f32[8,20,128,128]{3,2,1,0:T(8,128)}) fusion(f32[8,20,128,128]{3,2,1,0:T(8,128)} %fusion.65, pred[8,128,128]{2,1,0:T(8,128)(4,1)S(1)} %broadcast_and_fusion.2), kind=kOutput, calls=%fused_computation.109.clone.1 | output fusion | flops 18350208 | bytes 21184512 | tf_op jit(solution)/shard_map/while/body/eval_jaxpr/sub | solution.py:29
  425.4 6.7 %divide_reduce_fusion.5 = f32[8,20,128]{2,1,0:T(8,128)S(1)} fusion(f32[8,20,128,128]{3,2,1,0:T(8,128)} %get-tuple-element.231, f32[8,20,128]{2,1,0:T(8,128)S(1)} %broadcast_add_fusion.6), kind=kLoop, calls=%fused_computation.14.clone.1 | loop fusion | flops 5222400 | bytes 10649600 | tf_op jit(solution)/shard_map/while/body/eval_jaxpr/reduce_sum | solution.py:33
  434.2 17.3 %fusion.66 = (f32[8,20,128]{2,1,0:T(8,128)S(1)}, f32[8,20,128,128]{3,2,1,0:T(8,128)}) fusion(f32[8,20,128,128]{3,2,1,0:T(8,128)} %fusion.65, pred[8,128,128]{2,1,0:T(8,128)(4,1)S(1)} %broadcast_and_fusion.2), kind=kOutput, calls=%fused_computation.108.clone.1 | output fusion | flops 13107327 | bytes 21184512 | tf_op jit(solution)/shard_map/while/body/eval_jaxpr/sub | solution.py:35
  451.5 6.8 %divide_reduce_fusion.4 = f32[8,20,128]{2,1,0:T(8,128)S(1)} fusion(f32[8,20,128,128]{3,2,1,0:T(8,128)} %get-tuple-element.226, f32[8,20,128]{2,1,0:T(8,128)S(1)} %broadcast_add_fusion.5), kind=kLoop, calls=%fused_computation.15.clone.1 | loop fusion | flops 5222400 | bytes 10649600 | tf_op jit(solution)/shard_map/while/body/eval_jaxpr/reduce_sum | solution.py:39
  462.6 104.2 %reduce-scatter.2.cloned.1.call-done = f32[16,20,128]{2,0,1:T(8,128)} async-done(((f32[256,20,128]{2,0,1:T(8,128)}), f32[16,20,128]{2,0,1:T(8,128)}) %reduce-scatter.2.cloned.1.call-update) | async-done | bytes 163856 | tf_op jit(solution)/shard_map/reduce_scatter | solution.py:124
  (88 shorter events, 58.1 us)
Async XLA Ops:
  6.5 16.3 %copy-start = (bf16[1280,1280]{1,0:T(8,128)(2,1)S(1)}, bf16[1280,1280]{1,0:T(8,128)(2,1)}, u32[]{:S(2)}) copy-start(bf16[1280,1280]{1,0:T(8,128)(2,1)} %param.11) | copy-start | bytes 9830404
  15.4 17.7 %all-to-all-start = ((s32[16,1,2]{2,1,0:T(1,128)}), s32[16,1,2]{2,1,0:T(1,128)S(1)}, u32[]{:S(2)}, u32[]{:S(2)}) async-start(s32[16,1,2]{2,1,0:T(1,128)} %bitcast.4), calls=%async_computation | async-start | bytes 16384 | tf_op jit(solution)/shard_map/all_to_all | solution.py:70
  52.1 193.3 %all-to-all-start.1 = ((bf16[16,2,128,1280]{3,2,1,0:T(8,128)(2,1)}), bf16[16,2,128,1280]{3,2,1,0:T(8,128)(2,1)}, u32[]{:S(2)}, u32[]{:S(2)}) async-start(bf16[16,2,128,1280]{3,2,1,0:T(8,128)(2,1)} %broadcast_select_fusion.2), calls=%async_computation.1 | async-start | bytes 20971520 | tf_op jit(solution)/shard_map/all_to_all | solution.py:80
  58.2 508.6 %reduce-scatter.2.cloned.1.call-start = ((), (), s32[]{:S(2)}) async-start(), calls=%async_computation.3 | async-start | bytes 2785280 | tf_op jit(solution)/shard_map/reduce_scatter | solution.py:124
  245.4 213.2 %copy-start.2 = (s32[32]{0:T(128)S(1)}, s32[32]{0:T(128)}, u32[]{:S(2)}) copy-start(s32[32]{0:T(128)} %get-tuple-element.142) | copy-start | bytes 388
  245.4 213.2 %copy-start.3 = (pred[32]{0:T(512)(128)(4,1)S(1)}, pred[32]{0:T(512)(128)(4,1)}, u32[]{:S(2)}) copy-start(pred[32]{0:T(512)(128)(4,1)} %broadcast_compare_fusion) | copy-start | bytes 100
  458.6 109.8 %copy-start.1 = (bf16[1280,1280]{1,0:T(8,128)(2,1)S(1)}, bf16[1280,1280]{1,0:T(8,128)(2,1)}, u32[]{:S(2)}) copy-start(bf16[1280,1280]{1,0:T(8,128)(2,1)} %param.11) | copy-start | bytes 9830404
Sparse Core Ops, SparseCore 0:
  462.7 104.0 reduce-scatter.1
where the time goes:
time: 576 us; the launch traced here: 575 us
  waiting for transfers between devices  290 us (50%)
  other arithmetic  158 us (27%)
  local copies, waits for them, and re-layouts  54.9 us (10%)
  matrix products  45 us (8%)
  starting transfers between devices  13.5 us (2%)
  between operations  13.5 us (2%)
    all_to_all x1, waiting for transfers between devices, local(): lax.all_to_all(outgoing.reshape(owners, CAP, residues, channels), 'own',...  186 us
    reduce_scatter x1, waiting for transfers between devices, local(): lax.psum_scatter(spread, 'own', scatter_dimension=0, tiled=True)  104 us
    sub x3, other arithmetic, pair_mass(): col_exp = jnp.where(live, jnp.exp(masked - col_top), 0.0)  51.8 us
    sub x3, other arithmetic, pair_mass(): row_exp = jnp.where(live, jnp.exp(masked - row_top), 0.0)  49.2 us
    dot_general x3, matrix products, pair_mass(): jnp.einsum('bihe,bjhe->bhij', left, right, preferred_element_type=jnp.flo...  24.3 us
    gather x6, local copies, waits for them, and re-layouts, step(): partner = jnp.take(arrived, slot_place, axis=0)  21.9 us
    reduce_sum x3, other arithmetic, pair_mass(): to_query = jnp.sum(col_exp / col_total, axis=3)  20.3 us
    reduce_sum x3, other arithmetic, pair_mass(): to_partner = jnp.sum(row_exp / row_total, axis=2)  20.2 us
  transfers between devices with their start and end apart: 3, of which 2 were waited for; matrix products, arithmetic and copies ran while one was open for 2% of the time, Pallas kernels for 0%

commit v1 on v0

--- a/solution.py
+++ b/solution.py
@@ -1,13 +1,20 @@
+import functools
 import math
 
 import jax
 import jax.numpy as jnp
 from jax import lax
+from jax.experimental import pallas as pl
+from jax.experimental.pallas import tpu as pltpu
 from jax.sharding import PartitionSpec as P
 
 HEADS = 20
 CAP = 2
-
+HEAD = 64
+PLANE = 4
+UNROLL = 8
+LOW, HIGH = 2.0**-60, 2.0**60
+TILE = 256
 
 block_pairs = 8
 
@@ -41,7 +48,7 @@
     return (to_query / ratio[:, None, None], to_partner * ratio[:, None, None])
 
 
-def local(embeddings, lengths, proj_weight, slot_of, pairs):
+def local_any(embeddings, lengths, proj_weight, slot_of, pairs):
     per_device, residues, channels = embeddings.shape
     owners = lax.axis_size("own")
     own_index = lax.axis_index("own")
@@ -124,6 +131,309 @@
     return own_total + lax.psum_scatter(spread, "own", scatter_dimension=0, tiled=True)
 
 
+def exchange_kernel(owners, emb_ref, w_ref, main_ref, extra_ref, stage, send_sem, recv_main, recv_extra, fwd_sem, local_sem):
+    me = lax.axis_index("own")
+    planes = owners // PLANE
+    z, part = me // PLANE, me % PLANE
+    half = emb_ref.shape[0] // 2
+    wide = PLANE * HEAD
+
+    barrier = pltpu.get_barrier_semaphore()
+    for k in range(1, owners):
+        pl.semaphore_signal(
+            barrier, inc=1, device_id={"own": (me + k) % owners}, device_id_type=pl.DeviceIdType.MESH
+        )
+    pl.semaphore_wait(barrier, owners - 1)
+
+    low = lax.broadcasted_iota(jnp.int32, (TILE, 2 * HEAD), 1) < HEAD
+
+    def project(step, column):
+        @pl.loop(0, half // TILE)
+        def _(t):
+            row = pl.multiple_of(t * TILE, TILE)
+            weight = w_ref[:, pl.ds(column, wide)]
+            top = jnp.dot(emb_ref[pl.ds(row, TILE), :], weight, preferred_element_type=jnp.float32)
+            bottom = jnp.dot(
+                emb_ref[pl.ds(half + row, TILE), :], weight, preferred_element_type=jnp.float32
+            )
+            for g in range(wide // (2 * HEAD)):
+                a = top[:, 2 * HEAD * g : 2 * HEAD * (g + 1)]
+                b = bottom[:, 2 * HEAD * g : 2 * HEAD * (g + 1)]
+                even = jnp.where(low, a, pltpu.roll(b, HEAD, 1))
+                odd = jnp.where(low, pltpu.roll(a, HEAD, 1), b)
+                stage[step, 2 * g, pl.ds(row, TILE), :] = even.astype(jnp.bfloat16)
+                stage[step, 2 * g + 1, pl.ds(row, TILE), :] = odd.astype(jnp.bfloat16)
+
+    def remote(src, dst, send, recv, target):
+        return pltpu.make_async_remote_copy(
+            src_ref=src,
+            dst_ref=dst,
+            send_sem=send,
+            recv_sem=recv,
+            device_id={"own": target},
+            device_id_type=pl.DeviceIdType.MESH,
+        )
+
+    sent = []
+    locals_ = []
+    project(0, owners * HEAD)
+    for k in (2, 1, 3):
+        q = (z + k) % planes
+        copy = remote(
+            stage.at[0, q], extra_ref.at[me], send_sem.at[0, k], recv_extra.at[me], q * PLANE + part
+        )
+        copy.start()
+        sent.append(copy)
+    copy = pltpu.make_async_copy(stage.at[0, z], extra_ref.at[me], local_sem.at[0])
+    copy.start()
+    locals_.append(copy)
+    for j in range(1, PLANE):
+        peer = z * PLANE + (part + j) % PLANE
+        copy = remote(
+            stage.at[0, z], extra_ref.at[me], fwd_sem.at[0, j], recv_extra.at[me], peer
+        )
+        copy.start()
+        sent.append(copy)
+    for step, k in enumerate((2, 1, 3, 0), 1):
+        plane = (z + k) % planes
+        project(step, pl.multiple_of(plane * wide, wide))
+        for j in range(PLANE):
+            other = (part + j) % PLANE
+            if k == 0 and j == 0:
+                copy = pltpu.make_async_copy(stage.at[step, other], main_ref.at[me], local_sem.at[1])
+                copy.start()
+                locals_.append(copy)
+                continue
+            copy = remote(
+                stage.at[step, other],
+                main_ref.at[me],
+                send_sem.at[step, j],
+                recv_main.at[me],
+                plane * PLANE + other,
+            )
+            copy.start()
+            sent.append(copy)
+
+    def arrived(ref, sem, source):
+        remote(ref.at[source], ref.at[source], fwd_sem.at[0, 0], sem.at[source], (me + 1) % owners).wait_recv()
+
+    for k in (1, 3, 2):
+        source = (z + k) % planes * PLANE + part
+        arrived(extra_ref, recv_extra, source)
+        for j in range(1, PLANE):
+            peer = z * PLANE + (part + j) % PLANE
+            copy = remote(
+                extra_ref.at[source], extra_ref.at[source], fwd_sem.at[k, j], recv_extra.at[source], peer
+            )
+            copy.start()
+            sent.append(copy)
+    for k in range(planes):
+        for j in range(1, PLANE):
+            arrived(extra_ref, recv_extra, (z + k) % planes * PLANE + (part + j) % PLANE)
+    for k in range(1, owners):
+        arrived(main_ref, recv_main, (me + k) % owners)
+    for copy in locals_:
+        copy.wait()
+    for copy in sent:
+        copy.wait_send()
+
+
+def exchange(owners, emb, weight):
+    half = emb.shape[0] // 2
+    steps = owners // PLANE + 1
+    slab = jax.ShapeDtypeStruct((owners, half, 2 * HEAD), jnp.bfloat16)
+    return pl.pallas_call(
+        functools.partial(exchange_kernel, owners),
+        out_shape=(slab, slab),
+        in_specs=[pl.BlockSpec(memory_space=pltpu.VMEM)] * 2,
+        out_specs=(pl.BlockSpec(memory_space=pl.ANY),) * 2,
+        scratch_shapes=[
+            pltpu.VMEM((steps, PLANE, half, 2 * HEAD), jnp.bfloat16),
+            pltpu.SemaphoreType.DMA((steps, PLANE)),
+            pltpu.SemaphoreType.DMA((owners,)),
+            pltpu.SemaphoreType.DMA((owners,)),
+            pltpu.SemaphoreType.DMA((owners // PLANE, PLANE)),
+            pltpu.SemaphoreType.DMA((2,)),
+        ],
+        compiler_params=pltpu.CompilerParams(
+            collective_id=0, has_side_effects=True, vmem_limit_bytes=40 * 2**20
+        ),
+        cost_estimate=pl.CostEstimate(
+            flops=2 * emb.size * weight.shape[1], bytes_accessed=40 * 2**20, transcendentals=0
+        ),
+    )(emb, weight)
+
+
+def pairs_kernel(
+    per_device, pair_ref, slot_ref, len_ref, part_ref, main_ref, extra_ref, out_ref, table, row_len
+):
+    owners, half, lanes = main_ref.shape
+    residues = 2 * half // per_device
+    prots = slot_ref.shape[0]
+    pair_count = pair_ref.shape[0] // 2
+    share = pair_count // PLANE
+    scale = math.log2(math.e) / math.sqrt(HEAD)
+
+    @pl.loop(0, prots)
+    def _(p):
+        row_len[slot_ref[p]] = len_ref[p]
+
+    out_ref[...] = jnp.zeros_like(out_ref)
+    lane = lax.broadcasted_iota(jnp.int32, (residues, lanes), 1)
+    position = lax.broadcasted_iota(jnp.int32, (residues, lanes), 0)
+    low = lane < HEAD
+
+    @pl.loop(0, owners)
+    def _(source):
+        for p in range(per_device // 2):
+            m = main_ref[source, p * residues : (p + 1) * residues, :].astype(jnp.float32)
+            e = extra_ref[source, p * residues : (p + 1) * residues, :].astype(jnp.float32)
+            first = source * per_device + p
+            second = first + per_device // 2
+            one = jnp.where(low, m, pltpu.roll(e, HEAD, 1))
+            two = jnp.where(low, pltpu.roll(m, HEAD, 1), e)
+            table[first] = jnp.where(position < row_len[first], one, 0.0).astype(jnp.bfloat16)
+            table[second] = jnp.where(position < row_len[second], two, 0.0).astype(jnp.bfloat16)
+
+    small = lax.broadcasted_iota(jnp.int32, (16, lanes), 1)
+    top = lax.broadcasted_iota(jnp.int32, (16, lanes), 0) == 0
+
+    def facts(k):
+        a, b = pair_ref[2 * k], pair_ref[2 * k + 1]
+        return slot_ref[a], slot_ref[b], len_ref[a], len_ref[b]
+
+    def pick(row, extra):
+        left = table[row]
+        keep = low if not extra else jnp.logical_not(low)
+        return jnp.where(keep, left, jnp.zeros_like(left))
+
+    def inner(x, y):
+        return lax.dot_general(x, y, (((1,), (1,)), ((), ())), preferred_element_type=jnp.float32)
+
+    def outer(x, y):
+        return lax.dot_general(x, y, (((1,), (0,)), ((), ())), preferred_element_type=jnp.float32)
+
+    def two_parts(x):
+        high = x.astype(jnp.bfloat16).astype(jnp.float32)
+        return jnp.where(top, high, x - high).astype(jnp.bfloat16)
+
+    def ratio_of(number, n_a, n_b):
+        fa = jnp.full((1, lanes), n_a, jnp.int32).astype(jnp.float32)
+        fb = jnp.full((1, lanes), n_b, jnp.int32).astype(jnp.float32)
+        return fa / fb, fb / fa
+
+    def add(row, kind, value):
+        owner, place = row // per_device, row % per_device
+        out_ref[owner, kind, pl.ds(place, 1), :] += value
+
+    def fast(extra, ks, bad):
+        known = [facts(k) for k in ks]
+        scores = [inner(pick(ra, extra), table[rb]) for ra, rb, _, _ in known]
+        weights = [jnp.exp2(s * scale).astype(jnp.bfloat16) for s in scores]
+        live_i = [small < na for _, _, na, _ in known]
+        live_j = [small < nb for _, _, _, nb in known]
+        row_tot = [
+            inner(jnp.where(j, 1.0, 0.0).astype(jnp.bfloat16), w) for j, w in zip(live_j, weights)
+        ]
+        col_tot = [
+            outer(jnp.where(i, 1.0, 0.0).astype(jnp.bfloat16), w) for i, w in zip(live_i, weights)
+        ]
+        for i, j, r, c in zip(live_i, live_j, row_tot, col_tot):
+            fine_r = (r > LOW) & (r < HIGH)
+            fine_c = (c > LOW) & (c < HIGH)
+            bad = bad + jnp.where(i, jnp.where(fine_r, 0.0, 1.0), 0.0)
+            bad = bad + jnp.where(j, jnp.where(fine_c, 0.0, 1.0), 0.0)
+        r_inv = [two_parts(jnp.where(i, 1.0 / r, 0.0)) for i, r in zip(live_i, row_tot)]
+        c_inv = [two_parts(jnp.where(j, 1.0 / c, 0.0)) for j, c in zip(live_j, col_tot)]
+        to_b = [outer(r, w) for r, w in zip(r_inv, weights)]
+        to_a = [inner(c, w) for c, w in zip(c_inv, weights)]
+        for (ra, rb, na, nb), i, j, a, b in zip(known, live_i, live_j, to_a, to_b):
+            a_over_b, b_over_a = ratio_of(None, na, nb)
+            add(ra, int(extra), jnp.where(i[:1], (a[0:1] + a[1:2]) * a_over_b, 0.0))
+            add(rb, int(extra), jnp.where(j[:1], (b[0:1] + b[1:2]) * b_over_a, 0.0))
+        return bad
+
+    def mass(left, right, n_left, n_right):
+        live = (position < n_left) & (lane < n_right)
+        masked = jnp.where(live, inner(left, right) * scale, -1e30)
+        top_row = jnp.max(masked, axis=1, keepdims=True)
+        weight = jnp.where(live, jnp.exp2(masked - top_row), 0.0)
+        total = jnp.sum(weight, axis=1, keepdims=True)
+        total = total + jnp.where(position[:, :1] < n_left, 0.0, 1.0)
+        return jnp.sum(weight / total, axis=0, keepdims=True)
+
+    def safe(extra, k):
+        ra, rb, na, nb = facts(k)
+        left, right = pick(ra, extra), pick(rb, extra)
+        a_over_b, b_over_a = ratio_of(None, na, nb)
+        add(ra, int(extra), mass(right, left, nb, na) * a_over_b)
+        add(rb, int(extra), mass(left, right, na, nb) * b_over_a)
+
+    start = part_ref[0] * share
+    bad = jnp.zeros((16, lanes), jnp.float32)
+    bad = lax.fori_loop(
+        0,
+        pair_count // UNROLL,
+        lambda t, bad: fast(False, [t * UNROLL + u for u in range(UNROLL)], bad),
+        bad,
+    )
+    bad = lax.fori_loop(
+        0,
+        share // UNROLL,
+        lambda t, bad: fast(True, [start + t * UNROLL + u for u in range(UNROLL)], bad),
+        bad,
+    )
+
+    @pl.when(jnp.max(bad) > 0.0)
+    def _():
+        out_ref[...] = jnp.zeros_like(out_ref)
+
+        @pl.loop(0, pair_count)
+        def _(k):
+            safe(False, k)
+
+        @pl.loop(0, share)
+        def _(k):
+            safe(True, start + k)
+
+
+def pair_sums(per_device, pairs, slot_of, lengths, part, main, extra):
+    owners, half, lanes = main.shape
+    prots = slot_of.shape[0]
+    residues = 2 * half // per_device
+    smem = pl.BlockSpec(memory_space=pltpu.SMEM)
+    vmem = pl.BlockSpec(memory_space=pltpu.VMEM)
+    return pl.pallas_call(
+        functools.partial(pairs_kernel, per_device),
+        out_shape=jax.ShapeDtypeStruct((owners, 2, per_device, residues), jnp.float32),
+        in_specs=[smem] * 4 + [vmem] * 2,
+        out_specs=vmem,
+        scratch_shapes=[
+            pltpu.VMEM((prots, residues, lanes), jnp.bfloat16),
+            pltpu.SMEM((prots,), jnp.int32),
+        ],
+        compiler_params=pltpu.CompilerParams(vmem_limit_bytes=44 * 2**20),
+    )(pairs, slot_of, lengths, part, main, extra)
+
+
+def local_split(embeddings, lengths, proj_weight, slot_of, pairs):
+    per_device, residues, channels = embeddings.shape
+    owners = lax.axis_size("own")
+    all_pairs = lax.all_gather(pairs.reshape(-1), "own", tiled=True)
+    main, extra = exchange(owners, embeddings.reshape(per_device * residues, channels), proj_weight)
+    part = (lax.axis_index("own") % PLANE).reshape(1)
+    mass = pair_sums(per_device, all_pairs, slot_of, lengths, part, main, extra)
+    back = lax.all_to_all(mass, "own", split_axis=0, concat_axis=0, tiled=True)
+    first = back[:, 0]
+    rest = back[:, 1].reshape(owners // PLANE, PLANE, per_device, residues).sum(axis=1)
+    return jnp.concatenate([first, rest], axis=0).transpose(1, 0, 2)
+
+
+def split_by_heads(mesh):
+    owners = mesh.shape["own"]
+    return owners % PLANE == 0 and HEADS == owners + owners // PLANE and owners // PLANE == PLANE
+
+
 def solution(mesh):
     placed = (
         P(("groups", "own"), None, None),
@@ -133,7 +443,7 @@
         P(("groups", "own"), None),
     )
     return jax.shard_map(
-        local,
+        local_split if split_by_heads(mesh) else local_any,
         mesh=mesh,
         in_specs=placed,
         out_specs=P(("groups", "own"), None, None),

time: 576 us -> 385 us (0.67)
  Pallas kernels: 0 us -> 329 us
  waiting for transfers between devices: 290 us -> 0 us
  other arithmetic: 158 us -> 0.69 us
  local copies, waits for them, and re-layouts: 54.9 us -> 4.3 us
  blocking collectives: 0 us -> 49.8 us
  matrix products: 45 us -> 0 us
  starting transfers between devices: 13.5 us -> 0 us
  between operations: 13.5 us -> 0.71 us
    pallas_call x0 -> x2, Pallas kernels: none -> 329 us  [the longest x1 230 us: pair_sums(): pl.pallas_call(functools.partial(pairs_kernel, per_device), out_shape=jax...]
    all_to_all x2 -> x0, waiting for transfers between devices: 186 us -> none  [the longest x1 186 us: local(): lax.all_to_all(outgoing.reshape(owners, CAP, residues, channels), 'own',...]
    reduce_scatter x1 -> x0, waiting for transfers between devices: 104 us -> none  [local(): lax.psum_scatter(spread, 'own', scatter_dimension=0, tiled=True)]
    sub x6 -> x0, other arithmetic: 101 us -> none  [the longest x3 51.8 us: pair_mass(): col_exp = jnp.where(live, jnp.exp(masked - col_top), 0.0)]
    gather x17 -> x0, local copies, waits for them, and re-layouts: 53.6 us -> none  [the longest x6 21.9 us: step(): partner = jnp.take(arrived, slot_place, axis=0)]
    dot_general x11 -> x0, matrix products: 45 us -> none  [the longest x3 24.3 us: pair_mass(): jnp.einsum('bihe,bjhe->bhij', left, right, preferred_element_type=jnp.flo...]
    reduce_sum x8 -> x1, other arithmetic: 40.7 us -> 0.01 us  [local_split(): back[:, 1].reshape(owners // PLANE, PLANE, per_device, residues).sum(axis=1)]
    all_to_all x0 -> x1, blocking collectives: none -> 36.1 us  [local_split(): back = lax.all_to_all(mass, 'own', split_axis=0, concat_axis=0, tiled=True)]
  transfers between devices with their start and end apart: 3 -> 0, of which waited for: 2 -> 0; matrix products, arithmetic and copies ran while one was open for 2% -> 0% of each run, Pallas kernels for 0% -> 0%
where the time goes in v1:
time: 385 us; the launch traced here: 384 us
  Pallas kernels  329 us (85%)
  blocking collectives  49.8 us (13%)
  local copies, waits for them, and re-layouts  4.3 us (1%)
    pallas_call x1, Pallas kernels, pair_sums(): pl.pallas_call(functools.partial(pairs_kernel, per_device), out_shape=jax...  230 us
    pallas_call x1, Pallas kernels, exchange(): pl.pallas_call(functools.partial(exchange_kernel, owners), out_shape=(sla...  99.2 us
    all_to_all x1, blocking collectives, local_split(): back = lax.all_to_all(mass, 'own', split_axis=0, concat_axis=0, tiled=True)  36.1 us
    unnamed x1, blocking collectives  13.7 us

profile of v1, /device:TPU:0, one launch (start us, length us, event | category | flops | bytes accessed | tf_op | source)
XLA Modules:
  0.0 384.4 jit_solution(3905763466494851320)
XLA Ops:
  0.0 0.8 copy.7
  0.8 0.1 reshape.12
  0.9 1.2 dynamic-slice
  2.8 0.2 dynamic-update-slice
  3.0 13.7 %all-reduce.pair_ref = s32[768]{0:T(1024)S(1)} all-reduce(s32[768]{0:T(1024)S(1)} %dynamic-update-slice), channel_id=1, replica_groups=mesh['groups'=2,'own'=16] {'own'}, use_global_device_ids=true, to_apply=%add | all-reduce | flops 768 | bytes 6144
  16.7 0.0 copy-start.2
  16.7 1.9 copy-done.2
  18.7 0.0 copy-start
  18.7 0.0 copy-start.1
  18.7 99.2 %shard_map.55 = (bf16[16,1024,128]{2,1,0:T(8,128)(2,1)S(1)}, bf16[16,1024,128]{2,1,0:T(8,128)(2,1)S(1)}) custom-call(bf16[2048,1280]{1,0:T(8,128)(2,1)} %bitcast.11, bf16[1280,1280]{1,0:T(8,128)(2,1)S(1)} %copy-done.2), custom_call_target="tpu_custom_call" | custom-call | flops 6710886400 | bytes 41943040 | tf_op jit(solution)/shard_map/pallas_call | solution.py:245
  117.9 0.0 copy-done
  117.9 0.0 copy-done.1
  117.9 229.6 %shard_map.56 = f32[16,2,16,128]{3,2,1,0:T(8,128)S(1)} custom-call(s32[768]{0:T(1024)S(1)} %all-reduce.pair_ref, s32[256]{0:T(256)S(1)} %copy-done, s32[256]{0:T(256)S(1)} %copy-done.1, s32[1]{0:T(128)} %bitcast.1.part_ref, bf16[16,1024,128]{2,1,0:T(8,128)(2,1)S(1)} %get-tuple-element.7.main_ref, bf16[16,1024,128]{2,1,0:T(8,128)(2,1)S(1)} %get-tuple-element.8.extra_ref), custom_call_target="tpu_custom_call" | custom-call | tf_op jit(solution)/shard_map/pallas_call | solution.py:406
  347.6 36.1 %all_to_all.5 = f32[16,2,16,128]{3,2,1,0:T(8,128)S(1)} all-to-all(f32[16,2,16,128]{3,2,1,0:T(8,128)S(1)} %shard_map.56), channel_id=1, replica_groups=mesh['groups'=2,'own'=16] {'own'}, dimensions={0} | all-to-all | bytes 524288 | tf_op jit(solution)/shard_map/all_to_all | solution.py:426
  383.7 0.7 maximum_bitcast_fusion
  (3 shorter events, 0.0 us)
Async XLA Ops:
  16.7 1.9 copy-start.2
  18.7 99.3 %copy-start = (s32[256]{0:T(256)S(1)}, s32[256]{0:T(256)}, u32[]{:S(2)}) copy-start(s32[256]{0:T(256)} %slot_ref.1) | copy-start | bytes 3076
  18.7 99.3 %copy-start.1 = (s32[256]{0:T(256)S(1)}, s32[256]{0:T(256)}, u32[]{:S(2)}) copy-start(s32[256]{0:T(256)} %len_ref.1) | copy-start | bytes 3076

commit v2 on v1

--- a/solution.py
+++ b/solution.py
@@ -14,7 +14,8 @@
 PLANE = 4
 UNROLL = 8
 LOW, HIGH = 2.0**-60, 2.0**60
-TILE = 256
+GRANULE = 16
+LADDER = (22, 23, 24, 26, 32)
 
 block_pairs = 8
 
@@ -131,11 +132,14 @@
     return own_total + lax.psum_scatter(spread, "own", scatter_dimension=0, tiled=True)
 
 
-def exchange_kernel(owners, emb_ref, w_ref, main_ref, extra_ref, stage, send_sem, recv_main, recv_extra, fwd_sem, local_sem):
+def exchange_kernel(
+    owners, packed, w_ref, main_ref, extra_ref, stage, send_sem, recv_main, recv_extra, fwd_sem, local_sem
+):
     me = lax.axis_index("own")
     planes = owners // PLANE
     z, part = me // PLANE, me % PLANE
-    half = emb_ref.shape[0] // 2
+    half = packed.shape[0] // 2
+    tile = half // 2
     wide = PLANE * HEAD
 
     barrier = pltpu.get_barrier_semaphore()
@@ -145,24 +149,24 @@
         )
     pl.semaphore_wait(barrier, owners - 1)
 
-    low = lax.broadcasted_iota(jnp.int32, (TILE, 2 * HEAD), 1) < HEAD
+    low = lax.broadcasted_iota(jnp.int32, (tile, 2 * HEAD), 1) < HEAD
 
     def project(step, column):
-        @pl.loop(0, half // TILE)
+        @pl.loop(0, half // tile)
         def _(t):
-            row = pl.multiple_of(t * TILE, TILE)
+            row = pl.multiple_of(t * tile, tile)
             weight = w_ref[:, pl.ds(column, wide)]
-            top = jnp.dot(emb_ref[pl.ds(row, TILE), :], weight, preferred_element_type=jnp.float32)
+            top = jnp.dot(packed[pl.ds(row, tile), :], weight, preferred_element_type=jnp.float32)
             bottom = jnp.dot(
-                emb_ref[pl.ds(half + row, TILE), :], weight, preferred_element_type=jnp.float32
+                packed[pl.ds(half + row, tile), :], weight, preferred_element_type=jnp.float32
             )
             for g in range(wide // (2 * HEAD)):
                 a = top[:, 2 * HEAD * g : 2 * HEAD * (g + 1)]
                 b = bottom[:, 2 * HEAD * g : 2 * HEAD * (g + 1)]
                 even = jnp.where(low, a, pltpu.roll(b, HEAD, 1))
                 odd = jnp.where(low, pltpu.roll(a, HEAD, 1), b)
-                stage[step, 2 * g, pl.ds(row, TILE), :] = even.astype(jnp.bfloat16)
-                stage[step, 2 * g + 1, pl.ds(row, TILE), :] = odd.astype(jnp.bfloat16)
+                stage[step, 2 * g, pl.ds(row, tile), :] = even.astype(jnp.bfloat16)
+                stage[step, 2 * g + 1, pl.ds(row, tile), :] = odd.astype(jnp.bfloat16)
 
     def remote(src, dst, send, recv, target):
         return pltpu.make_async_remote_copy(
@@ -238,8 +242,28 @@
         copy.wait_send()
 
 
-def exchange(owners, emb, weight):
-    half = emb.shape[0] // 2
+def pack_kernel(source_ref, emb_ref, packed):
+    @pl.loop(0, packed.shape[0] // GRANULE, unroll=4)
+    def _(g):
+        start = pl.multiple_of(source_ref[g] * GRANULE, GRANULE)
+        here = pl.multiple_of(g * GRANULE, GRANULE)
+        packed[pl.ds(here, GRANULE), :] = emb_ref[pl.ds(start, GRANULE), :]
+
+
+def pack(half, source, emb):
+    return pl.pallas_call(
+        pack_kernel,
+        out_shape=jax.ShapeDtypeStruct((2 * half, emb.shape[1]), jnp.bfloat16),
+        in_specs=[
+            pl.BlockSpec(memory_space=pltpu.SMEM),
+            pl.BlockSpec(memory_space=pltpu.VMEM),
+        ],
+        out_specs=pl.BlockSpec(memory_space=pltpu.VMEM),
+        compiler_params=pltpu.CompilerParams(vmem_limit_bytes=20 * 2**20),
+    )(source, emb)
+
+
+def exchange(owners, half, kernel_id, emb, weight):
     steps = owners // PLANE + 1
     slab = jax.ShapeDtypeStruct((owners, half, 2 * HEAD), jnp.bfloat16)
     return pl.pallas_call(
@@ -256,44 +280,43 @@
             pltpu.SemaphoreType.DMA((2,)),
         ],
         compiler_params=pltpu.CompilerParams(
-            collective_id=0, has_side_effects=True, vmem_limit_bytes=40 * 2**20
+            collective_id=kernel_id, has_side_effects=True, vmem_limit_bytes=40 * 2**20
         ),
         cost_estimate=pl.CostEstimate(
-            flops=2 * emb.size * weight.shape[1], bytes_accessed=40 * 2**20, transcendentals=0
+            flops=4 * half * weight.size, bytes_accessed=40 * 2**20, transcendentals=0
         ),
     )(emb, weight)
 
 
 def pairs_kernel(
-    per_device, pair_ref, slot_ref, len_ref, part_ref, main_ref, extra_ref, out_ref, table, row_len
+    per_device, pair_ref, slot_ref, len_ref, start_ref, part_ref, main_ref, extra_ref, out_ref, table
 ):
     owners, half, lanes = main_ref.shape
-    residues = 2 * half // per_device
-    prots = slot_ref.shape[0]
+    residues = out_ref.shape[3]
     pair_count = pair_ref.shape[0] // 2
     share = pair_count // PLANE
     scale = math.log2(math.e) / math.sqrt(HEAD)
-
-    @pl.loop(0, prots)
-    def _(p):
-        row_len[slot_ref[p]] = len_ref[p]
 
     out_ref[...] = jnp.zeros_like(out_ref)
     lane = lax.broadcasted_iota(jnp.int32, (residues, lanes), 1)
     position = lax.broadcasted_iota(jnp.int32, (residues, lanes), 0)
     low = lane < HEAD
 
+    table[owners * 2 * half :, :] = jnp.zeros((residues, lanes), jnp.bfloat16)
+    strip = half // 2
+    low_strip = lax.broadcasted_iota(jnp.int32, (strip, lanes), 1) < HEAD
+
     @pl.loop(0, owners)
     def _(source):
-        for p in range(per_device // 2):
-            m = main_ref[source, p * residues : (p + 1) * residues, :].astype(jnp.float32)
-            e = extra_ref[source, p * residues : (p + 1) * residues, :].astype(jnp.float32)
-            first = source * per_device + p
-            second = first + per_device // 2
-            one = jnp.where(low, m, pltpu.roll(e, HEAD, 1))
-            two = jnp.where(low, pltpu.roll(m, HEAD, 1), e)
-            table[first] = jnp.where(position < row_len[first], one, 0.0).astype(jnp.bfloat16)
-            table[second] = jnp.where(position < row_len[second], two, 0.0).astype(jnp.bfloat16)
+        for p in range(half // strip):
+            m = main_ref[source, p * strip : (p + 1) * strip, :].astype(jnp.float32)
+            e = extra_ref[source, p * strip : (p + 1) * strip, :].astype(jnp.float32)
+            first = pl.multiple_of(source * 2 * half + p * strip, GRANULE)
+            second = pl.multiple_of(source * 2 * half + half + p * strip, GRANULE)
+            one = jnp.where(low_strip, m, pltpu.roll(e, HEAD, 1))
+            two = jnp.where(low_strip, pltpu.roll(m, HEAD, 1), e)
+            table[pl.ds(first, strip), :] = one.astype(jnp.bfloat16)
+            table[pl.ds(second, strip), :] = two.astype(jnp.bfloat16)
 
     small = lax.broadcasted_iota(jnp.int32, (16, lanes), 1)
     top = lax.broadcasted_iota(jnp.int32, (16, lanes), 0) == 0
@@ -302,8 +325,12 @@
         a, b = pair_ref[2 * k], pair_ref[2 * k + 1]
         return slot_ref[a], slot_ref[b], len_ref[a], len_ref[b]
 
+    def rows(row):
+        start = row // per_device * (2 * half) + start_ref[row] * GRANULE
+        return table[pl.ds(pl.multiple_of(start, GRANULE), residues), :]
+
     def pick(row, extra):
-        left = table[row]
+        left = rows(row)
         keep = low if not extra else jnp.logical_not(low)
         return jnp.where(keep, left, jnp.zeros_like(left))
 
@@ -328,7 +355,7 @@
 
     def fast(extra, ks, bad):
         known = [facts(k) for k in ks]
-        scores = [inner(pick(ra, extra), table[rb]) for ra, rb, _, _ in known]
+        scores = [inner(pick(ra, extra), rows(rb)) for ra, rb, _, _ in known]
         weights = [jnp.exp2(s * scale).astype(jnp.bfloat16) for s in scores]
         live_i = [small < na for _, _, na, _ in known]
         live_j = [small < nb for _, _, _, nb in known]
@@ -397,32 +424,65 @@
             safe(True, start + k)
 
 
-def pair_sums(per_device, pairs, slot_of, lengths, part, main, extra):
+def pair_sums(per_device, residues, pairs, slot_of, lengths, starts, part, main, extra):
     owners, half, lanes = main.shape
-    prots = slot_of.shape[0]
-    residues = 2 * half // per_device
     smem = pl.BlockSpec(memory_space=pltpu.SMEM)
     vmem = pl.BlockSpec(memory_space=pltpu.VMEM)
     return pl.pallas_call(
         functools.partial(pairs_kernel, per_device),
         out_shape=jax.ShapeDtypeStruct((owners, 2, per_device, residues), jnp.float32),
-        in_specs=[smem] * 4 + [vmem] * 2,
+        in_specs=[smem] * 5 + [vmem] * 2,
         out_specs=vmem,
         scratch_shapes=[
-            pltpu.VMEM((prots, residues, lanes), jnp.bfloat16),
-            pltpu.SMEM((prots,), jnp.int32),
+            pltpu.VMEM((owners * 2 * half + residues, lanes), jnp.bfloat16),
         ],
         compiler_params=pltpu.CompilerParams(vmem_limit_bytes=44 * 2**20),
-    )(pairs, slot_of, lengths, part, main, extra)
+    )(pairs, slot_of, lengths, starts, part, main, extra)
 
 
 def local_split(embeddings, lengths, proj_weight, slot_of, pairs):
     per_device, residues, channels = embeddings.shape
     owners = lax.axis_size("own")
-    all_pairs = lax.all_gather(pairs.reshape(-1), "own", tiled=True)
-    main, extra = exchange(owners, embeddings.reshape(per_device * residues, channels), proj_weight)
-    part = (lax.axis_index("own") % PLANE).reshape(1)
-    mass = pair_sums(per_device, all_pairs, slot_of, lengths, part, main, extra)
+    own = lax.axis_index("own")
+    full = per_device * residues // 2
+    ladder = [full * step // LADDER[-1] for step in LADDER]
+    row_ids = jnp.arange(owners * per_device, dtype=jnp.int32)
+    row_len = jnp.sum(jnp.where(slot_of[None, :] == row_ids[:, None], lengths[None, :], 0), axis=1)
+    count = ((row_len + GRANULE - 1) // GRANULE).reshape(owners, per_device)
+    place = jnp.arange(per_device, dtype=jnp.int32)
+    starts = jnp.sum(jnp.where(place[None, None, :] < place[None, :, None], count[:, None, :], 0), axis=2)
+    need = jnp.max(jnp.sum(count, axis=1))
+    sent = jnp.concatenate([pairs.reshape(-1), need.reshape(1)])
+    known = lax.all_gather(sent, ("groups", "own"))
+    known = known.reshape(lax.axis_size("groups"), owners, -1)
+    need = jnp.max(known[:, :, -1])
+    all_pairs = lax.dynamic_index_in_dim(known, lax.axis_index("groups"), 0, False)[:, :-1].reshape(-1)
+    my_start = lax.dynamic_index_in_dim(starts, own, 0, False)
+    my_count = lax.dynamic_index_in_dim(count, own, 0, False)
+    granules = jnp.arange(2 * full // GRANULE, dtype=jnp.int32)
+    offset = granules[:, None] - my_start[None, :]
+    source = jnp.sum(
+        jnp.where(
+            (offset >= 0) & (offset < my_count[None, :]),
+            offset + place[None, :] * (residues // GRANULE),
+            0,
+        ),
+        axis=1,
+    )
+    part = (own % PLANE).reshape(1)
+    rows = embeddings.reshape(per_device * residues, channels)
+
+    def branch(kernel_id, half):
+        def run():
+            main, extra = exchange(owners, half, kernel_id, pack(half, source, rows), proj_weight)
+            return pair_sums(
+                per_device, residues, all_pairs, slot_of, lengths, starts.reshape(-1), part, main, extra
+            )
+
+        return run
+
+    choice = sum((need * GRANULE > 2 * half).astype(jnp.int32) for half in ladder[:-1])
+    mass = lax.switch(choice, [branch(k, half) for k, half in enumerate(ladder)])
     back = lax.all_to_all(mass, "own", split_axis=0, concat_axis=0, tiled=True)
     first = back[:, 0]
     rest = back[:, 1].reshape(owners // PLANE, PLANE, per_device, residues).sum(axis=1)

time: 385 us -> 389 us (1.010)
  blocking collectives: 49.8 us -> 71.9 us
  Pallas kernels: 329 us -> 308 us
    unnamed x1, blocking collectives: 13.7 us -> 41.9 us
    pallas_call x1, Pallas kernels: 99.2 us -> 72.2 us  [exchange(): pl.pallas_call(functools.partial(exchange_kernel, owners), out_shape=(sla...]
    all_to_all x1, blocking collectives: 36.1 us -> 30 us  [local_split(): back = lax.all_to_all(mass, 'own', split_axis=0, concat_axis=0, tiled=True)]
where the time goes in v2:
time: 389 us; the launch traced here: 390 us
  Pallas kernels  308 us (79%)
  blocking collectives  71.9 us (18%)
  local copies, waits for them, and re-layouts  5.06 us (1%)
  other arithmetic  4.25 us (1%)
    pallas_call x1, Pallas kernels, pair_sums(): pl.pallas_call(functools.partial(pairs_kernel, per_device), out_shape=jax...  233 us
    pallas_call x1, Pallas kernels, exchange(): pl.pallas_call(functools.partial(exchange_kernel, owners), out_shape=(sla...  72.2 us
    unnamed x1, blocking collectives  41.9 us
    all_to_all x1, blocking collectives, local_split(): back = lax.all_to_all(mass, 'own', split_axis=0, concat_axis=0, tiled=True)  30 us

profile of v2, /device:TPU:0, one launch (start us, length us, event | category | flops | bytes accessed | tf_op | source)
XLA Modules:
  0.0 390.1 jit_solution(14156380704921383900)
XLA Ops:
  0.0 0.8 select_reduce_fusion
  0.8 0.1 sub.33
  0.9 0.1 fusion.7
  1.0 0.8 copy.12
  1.8 0.1 reshape.79
  1.9 0.6 reduce_max.18
  2.5 0.8 add_dynamic-update-slice_fusion
  3.4 41.9 %all-reduce = s32[1568]{0:T(1024)S(1)} all-reduce(s32[1568]{0:T(1024)S(1)} %add_dynamic-update-slice_fusion), channel_id=2, replica_groups=mesh['groups'=2,'own'=16] {'groups','own'}, use_global_device_ids=true, to_apply=%add | all-reduce | flops 1568 | bytes 12544
  45.3 0.1 reshape.81
  45.4 0.7 slice_reduce_fusion
  46.1 0.1 reshape.83
  46.9 0.3 select_reduce_fusion.1
  47.3 0.1 select_reduce_fusion.2
  47.3 312.1 %conditional.1 = (f32[16,2,16,128]{3,2,1,0:T(8,128)}) conditional(s32[]{:T(128)} %clamp.3, (s32[16,16]{1,0:T(8,128)S(1)}, s32[128]{0:T(128)S(1)}, bf16[2048,1280]{1,0:T(8,128)(2,1)}, bf16[1280,1280]{1,0:T(8,128)(2,1)}, s32[768]{0:T(1024)S(1)}, /*index=5*/s32[256]{0:T(256)}, s32[256]{0:T(256)}, s32[1]{0:T(128)}) %tuple.29, ...), branch_computations={%region_6.7_spmd, %region_7.8_spmd, %region_8.9_spmd, %region_9.10... | conditional | flops 6710886400 | bytes 122169552 | solution.py:485
  47.4 0.0 copy-start.23
  47.4 3.1 branch_1_fun.3.packed
  50.5 0.4 copy-done.23
  50.9 72.2 %branch_1_fun.4 = (bf16[16,736,128]{2,1,0:T(8,128)(2,1)S(1)}, bf16[16,736,128]{2,1,0:T(8,128)(2,1)S(1)}) custom-call(bf16[1472,1280]{1,0:T(8,128)(2,1)S(1)} %branch_1_fun.3.packed, bf16[1280,1280]{1,0:T(8,128)(2,1)S(1)} %copy-done.23), custom_call_target="tpu_custom_call" | custom-call | flops 4823449600 | bytes 41943040 | tf_op jit(solution)/shard_map/cond/branch_1_fun/pallas_call | solution.py:269
  123.0 1.6 copy-done.8
  124.6 0.1 reshape.69.start_ref
  124.7 1.8 copy-done.9
  126.6 232.9 %branch_1_fun.5 = f32[16,2,16,128]{3,2,1,0:T(8,128)} custom-call(s32[768]{0:T(1024)S(1)} %get-tuple-element.101.pair_ref, s32[256]{0:T(256)S(1)} %copy-done.18, s32[256]{0:T(256)S(1)} %copy-done.13, s32[256]{0:T(256)S(1)} %reshape.69.start_ref, s32[1]{0:T(128)} %get-tuple-element.105.part_ref, bf16[16,736,128]{2,1,0:T(8,128)(2,1)S(1)} %get-tuple-element.109.main_ref, ...), custom_call_target="tpu_custom_call" | custom-call | tf_op jit(solution)/shard_map/cond/branch_1_fun/pallas_call | solution.py:431
  359.4 30.0 %all_to_all.5 = f32[16,2,16,128]{3,2,1,0:T(8,128)S(1)} all-to-all(f32[16,2,16,128]{3,2,1,0:T(8,128)} %get-tuple-element.147), channel_id=1, replica_groups=mesh['groups'=2,'own'=16] {'own'}, dimensions={0} | all-to-all | bytes 524288 | tf_op jit(solution)/shard_map/all_to_all | solution.py:486
  389.5 0.7 maximum_bitcast_fusion
  (14 shorter events, 0.1 us)
Async XLA Ops:
  47.4 3.5 copy-start.23
  50.8 73.9 %copy-start.13 = (s32[256]{0:T(256)S(1)}, s32[256]{0:T(256)}, u32[]{:S(2)}) copy-start(s32[256]{0:T(256)} %get-tuple-element.103.len_ref) | copy-start | bytes 3076 | tf_op jit(solution)/shard_map/cond
  50.8 73.9 %copy-start.18 = (s32[256]{0:T(256)S(1)}, s32[256]{0:T(256)}, u32[]{:S(2)}) copy-start(s32[256]{0:T(256)} %get-tuple-element.102.slot_ref) | copy-start | bytes 3076 | tf_op jit(solution)/shard_map/cond
  123.0 1.6 copy-start.8
  124.7 1.9 copy-start.9
